TPU v7x, 32 devices: a whole 2x2x4 slice. The times are simulated.
32 devices in a mesh: groups: 2 (over y), dp: 2 (over core), chan: 8 (over z, x).
Axes of the slice: x: 2, y: 2, z: 4, core: 2. Of those that a mesh axis runs over, the one named last changes fastest.
Arguments:
- counts: int32 [4], P('groups'), parts along dimension 0, may hold values from 0 to 2, as said below
- inputs: bfloat16 [8, 1024, 8192], P(('groups', 'dp'), None, 'chan'), parts along dimension 0, may hold values from -6 to 6
- cotangent: bfloat16 [8, 1024, 8192], P(('groups', 'dp'), None, 'chan'), parts along dimension 0, may hold values from -6 to 6
- basis: float32 [128, 128], replicated, may hold values from -0.5 to 0.5
- eigvals: float32 [8192, 128], P('chan'), may hold values from 0.05 to 150
- query_context: bfloat16 [1024, 8192], P(None, 'chan'), may hold values from -6 to 6
- query_cotangent: bfloat16 [64, 8192], P(None, 'chan'), may hold values from -6 to 6
- query_pos: int32 [64], replicated, may hold values from 127 to 1023
Outputs:
- scores: float32 [8, 64], P(('groups', 'dp')), parts along dimension 0
There are 2 independent parts, one for each index of `groups`. A program takes and returns all parts, laid end to end along the dimension named above; an argument that names none is the same for every part. Nothing has to cross between parts.
Inputs may be any that keep to these rules, and one draw needn't show every extreme that they name: One of the two counts is 2, the other at most 1.
All inputs are finite; a program needn't handle non-finite values.
Results may differ from a plain program's by a relative error of at most 0.0003.
Values may be sent and summed in bfloat16 or wider, within the bound.
No kernel may reach another device: no remote copies, remote signals or barrier semaphores. Data moves between devices by JAX's collectives and lax.ppermute only.
A program may use at most 576 MiB of HBM per device.

v0:
```python
import jax
import jax.numpy as jnp
from jax import lax
from jax.sharding import PartitionSpec as P

damping = 0.1


def from_partner(value, axis, distance):
    mask = 2**distance
    pairs = [(source, source ^ mask) for source in range(lax.axis_size(axis))]
    return lax.ppermute(value, axis, pairs)


def window_grad(window_in, window_ct, tap_count):
    length_rows, chan_width = window_in.shape
    block_count = length_rows // tap_count
    current = window_in.reshape(block_count, tap_count, chan_width)
    previous = jnp.concatenate(
        [jnp.zeros((1, tap_count, chan_width), window_in.dtype), current[:-1]], 0
    )
    segment = jnp.concatenate([previous, current], 1)
    blocks = window_ct.reshape(block_count, tap_count, chan_width)
    outer_sum = jnp.einsum("bic,bjc->cij", blocks, segment, preferred_element_type=jnp.float32)
    flat_sum = outer_sum.reshape(chan_width, 2 * tap_count * tap_count)
    flat_sum = jnp.pad(flat_sum, ((0, 0), (0, tap_count)))
    skewed = flat_sum.reshape(chan_width, tap_count, 2 * tap_count + 1)
    summed = jnp.sum(skewed[:, :, 1 : tap_count + 1], axis=1)
    return summed[:, ::-1]


def body(counts, inputs, cotangent, basis, eigvals, query_context, query_cotangent, query_pos):
    capacity = inputs.shape[0]
    spare_rows = capacity // 2
    tap_count = basis.shape[0]
    chan_width = inputs.shape[2]
    query_count = query_pos.shape[0]
    row_index = query_pos[:, None] - jnp.arange(tap_count, dtype=jnp.int32)[None, :]
    context_rows = query_context[row_index]
    query_grad = context_rows.astype(jnp.float32) * query_cotangent.astype(jnp.float32)[:, None, :]
    query_rot = jnp.einsum("qkc,ka->qca", query_grad, basis, precision=lax.Precision.HIGHEST)
    weight = 1.0 / (eigvals + damping)
    query_probe = (query_rot * weight[None]).reshape(query_count, chan_width * tap_count)
    my_index = lax.axis_index("dp")
    my_count = counts[my_index]
    peer_count = counts[1 - my_index]
    upper_half = (my_count + peer_count + 1) // 2
    is_heavy = (my_count > peer_count) | (my_count == peer_count) & (my_index == 0)

    def own_window(position):
        safe_pos = jnp.clip(position, 0, capacity - 1)
        return (
            lax.dynamic_index_in_dim(inputs, safe_pos, 0, keepdims=False),
            lax.dynamic_index_in_dim(cotangent, safe_pos, 0, keepdims=False),
        )

    kept_count = jnp.where(is_heavy, upper_half, my_count)
    slab_start = jnp.minimum(kept_count, capacity - spare_rows)
    send_slab = jnp.stack(
        [
            lax.dynamic_slice_in_dim(inputs, slab_start, spare_rows, 0),
            lax.dynamic_slice_in_dim(cotangent, slab_start, spare_rows, 0),
        ]
    )
    arrived = from_partner(send_slab, "dp", 0)
    peer_start = jnp.minimum(upper_half, capacity - spare_rows)
    offset = jnp.where(is_heavy, 0, upper_half - peer_start)
    moved_count = jnp.where(is_heavy, 0, peer_count - upper_half)
    trip_count = kept_count + moved_count
    loop_length = (3 * capacity + 3) // 4

    def fetch_window(position):
        foreign_pos = jnp.clip(offset + position - kept_count, 0, spare_rows - 1)

        def from_peer(unused):
            return (
                lax.dynamic_index_in_dim(arrived[0], foreign_pos, 0, keepdims=False),
                lax.dynamic_index_in_dim(arrived[1], foreign_pos, 0, keepdims=False),
            )

        return lax.cond(position < kept_count, own_window, from_peer, position)

    def target_row(position):
        return jnp.where(position < kept_count, position, capacity + offset + position - kept_count)

    def window_work(position):
        window_in, window_ct = fetch_window(position)
        tap_grads = window_grad(window_in, window_ct, tap_count)
        rotated = jnp.dot(
            tap_grads, basis, precision=lax.Precision.HIGHEST, preferred_element_type=jnp.float32
        )
        part_raw = jnp.dot(
            query_probe,
            rotated.reshape(chan_width * tap_count),
            precision=lax.Precision.HIGHEST,
            preferred_element_type=jnp.float32,
        )
        part_norm = jnp.sum(rotated * rotated * weight)
        return (part_raw, part_norm)

    def no_work(position):
        return (jnp.zeros((query_count,), jnp.float32), jnp.zeros((), jnp.float32))

    def window_step(position, carry):
        raw_buf, norm_buf, live_buf = carry
        active = position < trip_count
        part_raw, part_norm = lax.cond(active, window_work, no_work, position)
        part_raw, part_norm = lax.psum((part_raw, part_norm), "chan")
        dest = jnp.clip(target_row(position), 0, capacity + spare_rows - 1)
        new_raw = lax.dynamic_update_slice_in_dim(raw_buf, part_raw[None], dest, 0)
        new_norm = lax.dynamic_update_slice_in_dim(norm_buf, part_norm[None], dest, 0)
        new_live = lax.dynamic_update_slice_in_dim(live_buf, jnp.ones((1,), jnp.float32), dest, 0)
        return (
            jnp.where(active, new_raw, raw_buf),
            jnp.where(active, new_norm, norm_buf),
            jnp.where(active, new_live, live_buf),
        )

    start_state = (
        jnp.zeros((capacity + spare_rows, query_count), jnp.float32),
        jnp.zeros((capacity + spare_rows,), jnp.float32),
        jnp.zeros((capacity + spare_rows,), jnp.float32),
    )
    raw_buf, norm_buf, live_buf = lax.fori_loop(0, loop_length, window_step, start_state)
    live_rows = live_buf > 0.5
    safe_norm = jnp.where(live_rows, norm_buf, jnp.float32(1.0))
    scores = jnp.where(live_rows[:, None], raw_buf / jnp.sqrt(safe_norm)[:, None], jnp.float32(0.0))
    result = scores[:capacity]
    returned = from_partner(scores[capacity:], "dp", 0)
    slot_ids = slab_start + jnp.arange(spare_rows, dtype=jnp.int32)
    take_back = is_heavy & (slot_ids >= kept_count) & (slot_ids < my_count)
    current = lax.dynamic_slice_in_dim(result, slab_start, spare_rows, 0)
    result = lax.dynamic_update_slice_in_dim(
        result, jnp.where(take_back[:, None], returned, current), slab_start, 0
    )
    return result


def solution(mesh):
    return jax.shard_map(
        body,
        mesh=mesh,
        in_specs=(
            P("groups"),
            P(("groups", "dp"), None, "chan"),
            P(("groups", "dp"), None, "chan"),
            P(),
            P("chan", None),
            P(None, "chan"),
            P(None, "chan"),
            P(),
        ),
        out_specs=P(("groups", "dp"), None),
        check_vma=False,
    )
```

profile of v0, /device:TPU:0, one launch (start us, length us, event | category | flops | bytes accessed | tf_op | source)
XLA Modules:
  0.0 1104.7 jit_solution(12271626891492119953)
XLA Ops:
  0.0 1.5 fusion.20
  6.3 2.7 dynamic-slice_bitcast_fusion.1
  9.0 2.4 pad_maximum_fusion
  11.4 0.5 collective-permute-start
  13.3 0.1 fusion.18
  13.4 35.3 %gather_fusion = bf16[8192,1024]{1,0:T(8,128)(2,1)} fusion(bf16[1024,1024]{1,0:T(8,128)(2,1)S(1)} %copy-done, s32[8192]{0:T(1024)S(1)} %fusion.18), kind=kCustom, calls=%fused_computation | custom fusion | bytes 33587200 | tf_op jit(solution)/shard_map/gather | solution.py:39
  48.7 23.2 %copy.22 = f32[64,128,1024]{1,2,0:T(8,128)} copy(bf16[64,128,1024]{2,1,0:T(8,128)(2,1)} %bitcast.62) | data formatting | bytes 50331648 | tf_op jit(solution)/shard_map/convert_element_type | solution.py:40
  71.9 0.1 add_divide_fusion
  72.0 33.0 %broadcast_multiply_fusion = f32[64,1024,128]{2,1,0:T(8,128)} fusion(f32[1024,128]{1,0:T(8,128)S(1)} %add_divide_fusion, f32[64,128,1024]{1,2,0:T(8,128)} %copy.22, f32[64,1024]{1,0:T(8,128)S(1)} %convert_element_type.22, f32[128,128]{1,0:T(8,128)S(1)} %copy-done.5), kind=kOutput, calls=%fused_computation.24 | convolution fusion | flops 12901679104 | bytes 67960832 | tf_op jit(solution)/shard_map/qkc,ka->qca/dot_general | solution.py:41
  105.1 31.9 %copy.29 = f32[8,8,1024,128]{3,1,2,0:T(8,128)} copy(f32[8,8,1024,128]{3,2,1,0:T(8,128)} %bitcast.60) | data formatting | bytes 67108864
  137.0 0.5 broadcast.68.clone
  137.5 0.6 broadcast.68
  138.1 0.6 broadcast_in_dim.53
  138.7 961.4 %while.19 = (s32[]{:T(128)}, f32[3,64]{1,0:T(4,128)}, f32[3]{0:T(128)}, f32[3]{0:T(128)}, s32[]{:T(128)}, /*index=5*/s32[]{:T(128)}, bf16[2,1,1024,1024]{3,2,1,0...) while((s32[]{:T(128)}, f32[3,64]{1,0:T(4,128)}, ...), condition=%wide.region_9.10_spmd, body=%wide.region_0.9_spmd.sunk | while | flops 868483200 | bytes 1094781312 | solution.py:124
  138.7 456.7 %conditional.3 = (f32[64]{0:T(128)}, f32[]{:T(128)}) conditional(s32[]{:T(128)} %convert_element_type.25, () %tuple.66, (s32[]{:T(128)}, s32[]{:T(128)}, bf16[2,1,1024,1024]{3,2,1,0:T(8,128)(2,1)}, bf16[2,1024,1024]{2,1,0:T(8,128)(2,1)}, bf16[2,1024,1024]{2,1,0:T(8,128)(2,1)}, /*index=5*/f32[128,128]{1,0:T(8,128)}, f32[64,131072]{1,0:T(8,128)}, ...), branch_computations={%region_1.1_spmd, %region_2.6_spmd} | conditional | flops 868483072 | bytes 1094779264 | solution.py:107
  138.7 8.5 conditional
  138.7 1.9 dynamic-slice_bitcast_fusion
  140.6 0.9 copy-done.4
  141.5 1.5 constant_dynamic-slice_fusion
  143.0 4.2 copy.26
  147.2 1.4 slice.20
  148.6 4.1 copy.18
  152.7 2.9 copy.23
  155.6 47.5 %fusion.2 = f32[1024,128,256]{2,1,0:T(8,128)} fusion(bf16[8,128,1024]{1,0,2:T(8,128)(2,1)} %get-tuple-element.366, bf16[7,128,1024]{1,0,2:T(8,128)(2,1)} %copy.18, bf16[8,128,1024]{1,0,2:T(8,128)(2,1)} %copy.23), kind=kOutput, calls=%fused_computation.8 | convolution fusion | flops 549453824 | bytes 140247040 | tf_op jit(solution)/shard_map/while/body/eval_jaxpr/cond/branch_1_fun/bic,bjc->cij/dot_general | solution.py:24
  203.1 126.2 %copy.24 = f32[1024,128,256]{0,2,1:T(8,128)} copy(f32[1024,128,256]{2,1,0:T(8,128)} %fusion.2) | data formatting | bytes 268435456 | tf_op jit(solution)/shard_map/while/body/eval_jaxpr/cond/branch_1_fun/reshape | solution.py:25
  329.3 86.3 %pad.6 = f32[1024,32896]{0,1:T(8,128)} pad(f32[1024,32768]{0,1:T(8,128)} %bitcast.6, f32[]{:T(128)} %constant.92.clone), padding=0_0x0_128 | pad | bytes 268959744 | tf_op jit(solution)/shard_map/while/body/eval_jaxpr/cond/branch_1_fun/jit(_pad)/pad | solution.py:26
  415.6 124.4 %reshape.86 = f32[1024,128,257]{0,2,1:T(8,128)} reshape(f32[1024,32896]{0,1:T(8,128)} %pad.6) | data formatting | bytes 269484032 | tf_op jit(solution)/shard_map/while/body/eval_jaxpr/cond/branch_1_fun/reshape | solution.py:27
  540.0 22.4 %slice_reduce_fusion = f32[1024,128]{0,1:T(8,128)S(1)} fusion(f32[1024,128,257]{0,2,1:T(8,128)} %reshape.86), kind=kLoop, calls=%fused_computation.4 | loop fusion | flops 16646144 | bytes 67633152 | tf_op jit(solution)/shard_map/while/body/eval_jaxpr/cond/branch_1_fun/reduce_sum | solution.py:28
  562.5 0.2 rev.3
  562.7 1.7 multiply_reduce_fusion
  564.4 30.3 %convolution_bitcast_fusion = f32[64]{0:T(128)} fusion(f32[131072,1]{0,1:T(1,128)S(1)} %bitcast.61, f32[64,131072]{1,0:T(8,128)} %get-tuple-element.342), kind=kOutput, calls=%fused_computation.13 | convolution fusion | flops 100663296 | bytes 34078976 | tf_op jit(solution)/shard_map/while/body/eval_jaxpr/cond/branch_1_fun/dot_general | solution.py:92
  595.4 23.8 %all-reduce.4 = (f32[1,64]{1,0:T(1,128)S(1)}, f32[1]{0:T(128)}) all-reduce(f32[1,64]{1,0:T(1,128)} %bitcast.52, f32[1]{0:T(128)} %bitcast.53), channel_id=1, replica_groups=mesh['groups'=2,'dp'=2,'chan'=8] {'chan'}, use_global_device_ids=true, to_apply=%region_7.7 | all-reduce | flops 65 | bytes 520 | tf_op jit(solution)/shard_map/while/body/eval_jaxpr/psum | solution.py:108
  619.2 0.7 broadcast_select_fusion.3
  619.9 0.8 select_dynamic-update-slice_fusion.4
  620.7 0.2 select_dynamic-update-slice_fusion.5
  620.8 1.3 select_n.160
  622.1 456.7 %conditional.3 = (f32[64]{0:T(128)}, f32[]{:T(128)}) conditional(s32[]{:T(128)} %convert_element_type.25, () %tuple.66, (s32[]{:T(128)}, s32[]{:T(128)}, bf16[2,1,1024,1024]{3,2,1,0:T(8,128)(2,1)}, bf16[2,1024,1024]{2,1,0:T(8,128)(2,1)}, bf16[2,1024,1024]{2,1,0:T(8,128)(2,1)}, /*index=5*/f32[128,128]{1,0:T(8,128)}, f32[64,131072]{1,0:T(8,128)}, ...), branch_computations={%region_1.1_spmd, %region_2.6_spmd} | conditional | flops 868483072 | bytes 1094779264 | solution.py:107
  622.1 8.5 conditional
  622.2 1.9 dynamic-slice_bitcast_fusion
  624.1 0.9 copy-done.4
  625.0 1.5 constant_dynamic-slice_fusion
  626.5 4.2 copy.26
  630.7 1.4 slice.20
  632.1 4.1 copy.18
  636.2 2.9 copy.23
  639.1 47.5 %fusion.2 = f32[1024,128,256]{2,1,0:T(8,128)} fusion(bf16[8,128,1024]{1,0,2:T(8,128)(2,1)} %get-tuple-element.366, bf16[7,128,1024]{1,0,2:T(8,128)(2,1)} %copy.18, bf16[8,128,1024]{1,0,2:T(8,128)(2,1)} %copy.23), kind=kOutput, calls=%fused_computation.8 | convolution fusion | flops 549453824 | bytes 140247040 | tf_op jit(solution)/shard_map/while/body/eval_jaxpr/cond/branch_1_fun/bic,bjc->cij/dot_general | solution.py:24
  686.6 126.2 %copy.24 = f32[1024,128,256]{0,2,1:T(8,128)} copy(f32[1024,128,256]{2,1,0:T(8,128)} %fusion.2) | data formatting | bytes 268435456 | tf_op jit(solution)/shard_map/while/body/eval_jaxpr/cond/branch_1_fun/reshape | solution.py:25
  812.8 86.3 %pad.6 = f32[1024,32896]{0,1:T(8,128)} pad(f32[1024,32768]{0,1:T(8,128)} %bitcast.6, f32[]{:T(128)} %constant.92.clone), padding=0_0x0_128 | pad | bytes 268959744 | tf_op jit(solution)/shard_map/while/body/eval_jaxpr/cond/branch_1_fun/jit(_pad)/pad | solution.py:26
  899.1 124.4 %reshape.86 = f32[1024,128,257]{0,2,1:T(8,128)} reshape(f32[1024,32896]{0,1:T(8,128)} %pad.6) | data formatting | bytes 269484032 | tf_op jit(solution)/shard_map/while/body/eval_jaxpr/cond/branch_1_fun/reshape | solution.py:27
  1023.5 22.4 %slice_reduce_fusion = f32[1024,128]{0,1:T(8,128)S(1)} fusion(f32[1024,128,257]{0,2,1:T(8,128)} %reshape.86), kind=kLoop, calls=%fused_computation.4 | loop fusion | flops 16646144 | bytes 67633152 | tf_op jit(solution)/shard_map/while/body/eval_jaxpr/cond/branch_1_fun/reduce_sum | solution.py:28
  1046.0 0.2 rev.3
  1046.2 1.7 multiply_reduce_fusion
  1047.9 30.3 %convolution_bitcast_fusion = f32[64]{0:T(128)} fusion(f32[131072,1]{0,1:T(1,128)S(1)} %bitcast.61, f32[64,131072]{1,0:T(8,128)} %get-tuple-element.342), kind=kOutput, calls=%fused_computation.13 | convolution fusion | flops 100663296 | bytes 34078976 | tf_op jit(solution)/shard_map/while/body/eval_jaxpr/cond/branch_1_fun/dot_general | solution.py:92
  1078.9 18.3 %all-reduce.4 = (f32[1,64]{1,0:T(1,128)S(1)}, f32[1]{0:T(128)}) all-reduce(f32[1,64]{1,0:T(1,128)} %bitcast.52, f32[1]{0:T(128)} %bitcast.53), channel_id=1, replica_groups=mesh['groups'=2,'dp'=2,'chan'=8] {'chan'}, use_global_device_ids=true, to_apply=%region_7.7 | all-reduce | flops 65 | bytes 520 | tf_op jit(solution)/shard_map/while/body/eval_jaxpr/psum | solution.py:108
  1097.2 0.7 broadcast_select_fusion.3
  1097.8 0.8 select_dynamic-update-slice_fusion.4
  1098.7 0.2 select_dynamic-update-slice_fusion.5
  1098.8 1.3 select_n.160
  1100.1 0.8 broadcast_compare_fusion
  1100.9 0.7 select_sqrt_fusion
  1101.5 0.7 divide_select_fusion
  1102.3 0.0 collective-permute-start.1
  1102.4 1.1 collective-permute-done.1
  1103.5 1.3 dynamic_update_slice.12
  (47 shorter events, 0.1 us)
Async XLA Ops:
  0.0 13.3 %copy-start = (bf16[1024,1024]{1,0:T(8,128)(2,1)S(1)}, bf16[1024,1024]{1,0:T(8,128)(2,1)}, u32[]{:S(2)}) copy-start(bf16[1024,1024]{1,0:T(8,128)(2,1)} %param.19) | copy-start | bytes 6291460
  9.0 4.2 copy-start.8
  9.0 4.2 copy-start.14
  11.4 125.6 %collective-permute-start = (bf16[2,1,1024,1024]{3,2,1,0:T(8,128)(2,1)}, bf16[2,1,1024,1024]{3,2,1,0:T(8,128)(2,1)}, u32[]{:S(2)}, u32[]{:S(2)}) collective-permute-start(bf16[2,1,1024,1024]{3,2,1,0:T(8,128)(2,1)} %pad_maximum_fusion), channel_id=1, source_target_pairs={{0,8},{8,0},{1,9},{9,1},{2,10},{10,2},{3,11},{11,3},{4,12},{12,4},... | collective-permute-start | bytes 12582920 | tf_op jit(solution)/shard_map/ppermute | solution.py:12
  48.7 23.2 %copy-start.7 = (f32[1024,128]{1,0:T(8,128)S(1)}, f32[1024,128]{1,0:T(8,128)}, u32[]{:S(2)}) copy-start(f32[1024,128]{1,0:T(8,128)} %param.18) | copy-start | bytes 1572868
  48.7 23.3 %copy-start.5 = (f32[128,128]{1,0:T(8,128)S(1)}, f32[128,128]{1,0:T(8,128)}, u32[]{:S(2)}) copy-start(f32[128,128]{1,0:T(8,128)} %param.17) | copy-start | bytes 196612
  72.0 33.1 %copy-start.2 = (f32[1024,128]{1,0:T(8,128)}, f32[1024,128]{1,0:T(8,128)S(1)}, u32[]{:S(2)}) copy-start(f32[1024,128]{1,0:T(8,128)S(1)} %add_divide_fusion) | copy-start | bytes 1572868
  138.7 481.2 %copy-start.9 = (f32[3]{0:T(128)S(1)}, f32[3]{0:T(128)}, u32[]{:S(2)}) copy-start(f32[3]{0:T(128)} %get-tuple-element.516) | copy-start | bytes 40 | tf_op jit(solution)/shard_map/while
  138.7 482.0 %copy-start.11 = (f32[3]{0:T(128)S(1)}, f32[3]{0:T(128)}, u32[]{:S(2)}) copy-start(f32[3]{0:T(128)} %get-tuple-element.517) | copy-start | bytes 40 | tf_op jit(solution)/shard_map/while
  138.7 2.8 copy-start.4
  540.0 22.7 %copy-start.3 = (f32[1024,128]{1,0:T(8,128)S(1)}, f32[1024,128]{1,0:T(8,128)}, u32[]{:S(2)}) copy-start(f32[1024,128]{1,0:T(8,128)} %get-tuple-element.343) | copy-start | bytes 1572868 | tf_op jit(solution)/shard_map/while/body/eval_jaxpr/cond
  540.0 22.7 %copy-start.6 = (f32[128,128]{1,0:T(8,128)S(1)}, f32[128,128]{1,0:T(8,128)}, u32[]{:S(2)}) copy-start(f32[128,128]{1,0:T(8,128)} %get-tuple-element.341) | copy-start | bytes 196612 | tf_op jit(solution)/shard_map/while/body/eval_jaxpr/cond
  620.7 1.4 copy-start.10
  620.8 1.3 copy-start.12
  622.1 475.7 %copy-start.9 = (f32[3]{0:T(128)S(1)}, f32[3]{0:T(128)}, u32[]{:S(2)}) copy-start(f32[3]{0:T(128)} %get-tuple-element.516) | copy-start | bytes 40 | tf_op jit(solution)/shard_map/while
  622.1 476.5 %copy-start.11 = (f32[3]{0:T(128)S(1)}, f32[3]{0:T(128)}, u32[]{:S(2)}) copy-start(f32[3]{0:T(128)} %get-tuple-element.517) | copy-start | bytes 40 | tf_op jit(solution)/shard_map/while
  622.2 2.8 copy-start.4
  1023.5 22.7 %copy-start.3 = (f32[1024,128]{1,0:T(8,128)S(1)}, f32[1024,128]{1,0:T(8,128)}, u32[]{:S(2)}) copy-start(f32[1024,128]{1,0:T(8,128)} %get-tuple-element.343) | copy-start | bytes 1572868 | tf_op jit(solution)/shard_map/while/body/eval_jaxpr/cond
  1023.5 22.7 %copy-start.6 = (f32[128,128]{1,0:T(8,128)S(1)}, f32[128,128]{1,0:T(8,128)}, u32[]{:S(2)}) copy-start(f32[128,128]{1,0:T(8,128)} %get-tuple-element.341) | copy-start | bytes 196612 | tf_op jit(solution)/shard_map/while/body/eval_jaxpr/cond
  1098.6 1.4 copy-start.10
  1098.8 1.3 copy-start.12
  1100.1 4.6 copy-start.1
  1102.3 1.1 collective-permute-start.1
  1102.4 1.1 copy-start.13
where the time goes:
time: 1110 us; the launch traced here: 1100 us
  local copies, waits for them, and re-layouts  808 us (73%)
  matrix products  192 us (17%)
  other arithmetic  52.9 us (5%)
  blocking collectives  42.2 us (4%)
    reshape x2, local copies, waits for them, and re-layouts, window_grad(): flat_sum = outer_sum.reshape(chan_width, 2 * tap_count * tap_count)  252 us
    reshape x2, local copies, waits for them, and re-layouts, window_grad(): skewed = flat_sum.reshape(chan_width, tap_count, 2 * tap_count + 1)  249 us
    pad x2, local copies, waits for them, and re-layouts, window_grad(): flat_sum = jnp.pad(flat_sum, ((0, 0), (0, tap_count)))  173 us
    dot_general x2, matrix products, window_grad(): jnp.einsum('bic,bjc->cij', blocks, segment, preferred_element_type=jnp.fl...  94.9 us
    dot_general x2, matrix products, window_work(): jnp.dot(query_probe, rotated.reshape(chan_width * tap_count), precision=l...  60.6 us
    reduce_sum x2, other arithmetic, window_grad(): summed = jnp.sum(skewed[:, :, 1:tap_count + 1], axis=1)  44.9 us
    psum x2, blocking collectives, window_step(): part_raw, part_norm = lax.psum((part_raw, part_norm), 'chan')  42.2 us
    gather x1, local copies, waits for them, and re-layouts, body(): context_rows = query_context[row_index]  35.3 us
  transfers between devices with their start and end apart: 2, of which 1 were waited for; matrix products, arithmetic and copies ran while one was open for 11% of the time, Pallas kernels for 0%

commit v1 on v0

v1 whole, which is shorter than its diff:
```python
import functools

import jax
import jax.numpy as jnp
import ml_dtypes
import numpy as np
from jax import lax
from jax.experimental import pallas as pl
from jax.experimental.pallas import tpu as pltpu
from jax.sharding import PartitionSpec as P

damping = 0.1
f32 = jnp.float32
bf16 = jnp.bfloat16


def transform_tables(taps):
    freq = np.arange(taps)
    angle = np.pi / taps * np.arange(taps)[:, None] * (freq + 0.5)[None, :]
    sign = np.where(freq % 2 == 0, 1.0, -1.0)
    real, imag = np.cos(angle), -np.sin(angle)
    forward = []
    for table in (np.concatenate([real, imag], 1), np.concatenate([sign * imag, -sign * real], 1)):
        high = table.astype(ml_dtypes.bfloat16)
        low = (table - high.astype(np.float64)).astype(ml_dtypes.bfloat16)
        forward.append(np.concatenate([high, low], 0))
    inverse = np.concatenate([np.sin(angle) * sign, np.cos(angle) * sign], 1).T / taps
    return np.stack(forward), inverse.astype(np.float32)


def split(value):
    high = value.astype(bf16)
    return high, (value - high.astype(f32)).astype(bf16)


def dot(a, b):
    return jnp.dot(a, b, preferred_element_type=f32)


def dot_nt(a, b):
    return lax.dot_general(a, b, (((1,), (1,)), ((), ())), preferred_element_type=f32)


def local_kernel(
    counts_hbm, pos_hbm, x_hbm, g_hbm, basis_hbm, eig_hbm, ctx_hbm, qct_hbm, fwd_hbm, inv_hbm, out_ref,
    xbuf, gbuf, ctxbuf, eigbuf, basisbuf, qctbuf, fwd, inv,
    x_turned, g_turned, rot_mat, back, vbuf, ctxf, qctf, raw, norm, counts_ref, pos_ref, sems, wsems,
):
    capacity, cb_count, length, cb = xbuf.shape
    taps = basisbuf.shape[0]
    queries = pos_ref.shape[0]
    blocks = length // taps
    tiles = cb // 128

    def columns(c):
        return pl.ds(c * cb, cb)

    scalars = [
        pltpu.make_async_copy(counts_hbm, counts_ref, sems.at[5 + cb_count]),
        pltpu.make_async_copy(pos_hbm, pos_ref, sems.at[6 + cb_count]),
    ]
    small = [
        pltpu.make_async_copy(fwd_hbm, fwd, sems.at[0]),
        pltpu.make_async_copy(basis_hbm, basisbuf, sems.at[1]),
        pltpu.make_async_copy(inv_hbm, inv, sems.at[2]),
        pltpu.make_async_copy(qct_hbm, qctbuf, sems.at[3]),
        pltpu.make_async_copy(eig_hbm, eigbuf, sems.at[4]),
    ]
    ctx_copies = [
        pltpu.make_async_copy(ctx_hbm.at[:, columns(c)], ctxbuf.at[c], sems.at[5 + c]) for c in range(cb_count)
    ]

    def window_copies(s, c):
        return (
            pltpu.make_async_copy(x_hbm.at[s, :, columns(c)], xbuf.at[s, c], wsems.at[0, s, c]),
            pltpu.make_async_copy(g_hbm.at[s, :, columns(c)], gbuf.at[s, c], wsems.at[1, s, c]),
        )

    for copy in scalars + small[:3]:
        copy.start()
    scalars[0].wait()
    count = counts_ref[lax.axis_index("dp")]
    for c in range(cb_count):
        for s in range(capacity):
            @pl.when(s < count)
            def _():
                for copy in window_copies(s, c):
                    copy.start()
            if c == 0 and s == 0:
                for copy in small[3:]:
                    copy.start()
        ctx_copies[c].start()

    raw[...] = jnp.zeros_like(raw)
    norm[...] = jnp.zeros_like(norm)
    for copy in small[:3]:
        copy.wait()

    base_hi, base_lo = split(basisbuf[...])
    inv_hi, inv_lo = split(inv[...])
    rot_hi, rot_lo = split(dot(inv_hi, base_hi) + (dot(inv_hi, base_lo) + dot(inv_lo, base_hi)))
    rot_mat[...] = jnp.concatenate([rot_hi, rot_lo], 1)
    row = lax.broadcasted_iota(jnp.int32, (taps, taps), 0)
    col = lax.broadcasted_iota(jnp.int32, (taps, taps), 1)
    flip = (row + col == taps - 1).astype(bf16)
    flip_hi = dot(flip, base_hi).astype(bf16)
    back[...] = jnp.concatenate([flip_hi, flip_hi, dot(flip, base_lo).astype(bf16)], 1)
    for copy in small[3:] + scalars[1:]:
        copy.wait()
    for t in range(cb_count * tiles):
        qctf[t] = qctbuf[:, t * 128:(t + 1) * 128].astype(f32)

    rows = 32

    def cross(first):
        def stack(parity):
            parts = []
            for b in range(blocks):
                turned = x_turned if b % 2 == parity else g_turned
                parts.append(turned[first:first + rows, b * taps:(b + 1) * taps])
            both = jnp.concatenate(parts, 0)
            return jnp.concatenate([both, both], 1)

        spectra = [dot(stack(0), fwd[0]), dot(stack(1), fwd[1])]

        def parts_of(array, b):
            block = spectra[b % 2 if array == 0 else 1 - b % 2][b * rows:(b + 1) * rows]
            return block[:, :taps], block[:, taps:]

        for b in range(blocks):
            x_re, x_im = parts_of(0, b)
            g_re, g_im = parts_of(1, b)
            if b == 0:
                t_re, t_im = -x_re, -x_im
            elif b % 2:
                t_re, t_im = prev_re + x_re, prev_im + x_im
            else:
                t_re, t_im = prev_re - x_re, prev_im - x_im
            add_re = g_re * t_re + g_im * t_im
            add_im = g_im * t_re - g_re * t_im
            sum_re = add_re if b == 0 else sum_re + add_re
            sum_im = add_im if b == 0 else sum_im + add_im
            prev_re, prev_im = x_re, x_im
        return jnp.concatenate([sum_re, sum_im], 1)

    def filters(s, c):
        x_turned[...] = xbuf[s, c].T
        g_turned[...] = gbuf[s, c].T
        high, low = split(jnp.concatenate([cross(first) for first in range(0, cb, rows)], 0))
        twice = dot(high, rot_mat[...])
        rotated = twice[:, :taps] + (twice[:, taps:] + dot(low, rot_mat[:, :taps]))
        scaled = rotated / (eigbuf[pl.ds(pl.multiple_of(c * cb, cb), cb), :] + damping)
        norm[s] += jnp.sum((scaled * rotated).reshape(cb // 8, 8, taps), 0)
        high, low = split(scaled)
        turned = dot_nt(back[:, :2 * taps], jnp.concatenate([high, low], 1)) + dot_nt(back[:, 2 * taps:], high)
        for t in range(tiles):
            vbuf[s, c * tiles + t] = turned[:, t * 128:(t + 1) * 128]

    for c in range(cb_count):
        for s in range(capacity):
            @pl.when(s < count)
            def _():
                for copy in window_copies(s, c):
                    copy.wait()
        ctx_copies[c].wait()

        def filter_step(s, unused):
            filters(s, c)
            return unused

        lax.fori_loop(0, count, filter_step, 0)

    per_iter = min(16, queries)

    def probes(windows):
        def tile_step(t, unused):
            c, part_of = t // tiles, t % tiles
            for k in range(tiles):
                @pl.when(part_of == k)
                def _():
                    ctxf[...] = ctxbuf[c, :, k * 128:(k + 1) * 128].astype(f32)

            def probe(i, unused):
                filt = [vbuf[s, t] for s in range(windows)]
                for u in range(per_iter):
                    q = i * per_iter + u
                    start = jnp.clip(pos_ref[q] - (taps - 1), 0, length - taps)
                    piece = ctxf[pl.ds(start, taps), :]
                    cotangent = qctf[t, pl.ds(q, 1), :]
                    for s in range(windows):
                        part = jnp.sum((piece * filt[s]).reshape(taps // 8, 8, 128), 0)
                        raw[s, q] += part * cotangent
                return unused

            lax.fori_loop(0, queries // per_iter, probe, 0)
            return unused

        lax.fori_loop(0, cb_count * tiles, tile_step, 0)

    for windows in range(1, capacity + 1):
        @pl.when(count == windows)
        def _():
            probes(windows)

    for s in range(capacity):
        per_query = jnp.sum(raw[s], 1)
        lane_one = (lax.broadcasted_iota(jnp.int32, (1, 128), 1) == 0).astype(f32)
        own = jnp.where(s < count, jnp.sum(norm[s], 0, keepdims=True), lane_one)
        table = jnp.concatenate([per_query, jnp.broadcast_to(own, (128 - queries, 128))], 0)
        out_ref[pl.ds(s, 1), :] = jnp.sum(table.T, 0, keepdims=True)


def local_sums(counts, inputs, cotangent, basis, eigvals, query_context, query_cotangent, query_pos):
    capacity, length, width = inputs.shape
    taps = basis.shape[0]
    queries = query_pos.shape[0]
    cb = min(256, width)
    cb_count, tiles = width // cb, cb // 128
    forward, inverse = transform_tables(taps)
    hbm = pl.BlockSpec(memory_space=pl.ANY)
    return pl.pallas_call(
        local_kernel,
        out_shape=jax.ShapeDtypeStruct((capacity, 128), f32),
        in_specs=[hbm] * 10,
        out_specs=pl.BlockSpec(memory_space=pltpu.VMEM),
        scratch_shapes=[
            pltpu.VMEM((capacity, cb_count, length, cb), bf16),
            pltpu.VMEM((capacity, cb_count, length, cb), bf16),
            pltpu.VMEM((cb_count, length, cb), bf16),
            pltpu.VMEM((width, taps), f32),
            pltpu.VMEM((taps, taps), f32),
            pltpu.VMEM((queries, width), bf16),
            pltpu.VMEM((2, 2 * taps, 2 * taps), bf16),
            pltpu.VMEM((2 * taps, taps), f32),
            pltpu.VMEM((cb, length), bf16),
            pltpu.VMEM((cb, length), bf16),
            pltpu.VMEM((2 * taps, 2 * taps), bf16),
            pltpu.VMEM((taps, 3 * taps), bf16),
            pltpu.VMEM((capacity, cb_count * tiles, taps, 128), f32),
            pltpu.VMEM((length, 128), f32),
            pltpu.VMEM((cb_count * tiles, queries, 128), f32),
            pltpu.VMEM((capacity, queries, 8, 128), f32),
            pltpu.VMEM((capacity, 8, 128), f32),
            pltpu.SMEM(counts.shape, jnp.int32),
            pltpu.SMEM((queries,), jnp.int32),
            pltpu.SemaphoreType.DMA((7 + cb_count,)),
            pltpu.SemaphoreType.DMA((2, capacity, cb_count)),
        ],
        compiler_params=pltpu.CompilerParams(vmem_limit_bytes=62 * 1024 * 1024),
        cost_estimate=pl.CostEstimate(flops=4 * 10**9, bytes_accessed=11 * 2**20, transcendentals=0),
    )(
        counts, query_pos, inputs, cotangent, basis, eigvals, query_context, query_cotangent,
        jnp.asarray(forward), jnp.asarray(inverse),
    )


def sum_over(value, axis):
    size = lax.axis_size(axis)
    mask = 1
    while mask < size:
        value = value + lax.ppermute(value, axis, [(i, i ^ mask) for i in range(size)])
        mask *= 2
    return value


def body(counts, inputs, cotangent, basis, eigvals, query_context, query_cotangent, query_pos):
    capacity = inputs.shape[0]
    queries = query_pos.shape[0]
    sums = local_sums(counts, inputs, cotangent, basis, eigvals, query_context, query_cotangent, query_pos)
    sums = sum_over(sums, "chan")
    return sums[:, :queries] / jnp.sqrt(sums[:, queries:queries + 1])


def solution(mesh):
    return jax.shard_map(
        body,
        mesh=mesh,
        in_specs=(
            P("groups"),
            P(("groups", "dp"), None, "chan"),
            P(("groups", "dp"), None, "chan"),
            P(),
            P("chan", None),
            P(None, "chan"),
            P(None, "chan"),
            P(),
        ),
        out_specs=P(("groups", "dp"), None),
        check_vma=False,
    )
```

time: 1110 us -> 35.4 us (0.03)
  local copies, waits for them, and re-layouts: 808 us -> 0.19 us
  matrix products: 192 us -> 0 us
  other arithmetic: 52.9 us -> 1.34 us
  blocking collectives: 42.2 us -> 0 us
  Pallas kernels: 0 us -> 20.6 us
    reshape x6 -> x0, local copies, waits for them, and re-layouts: 507 us -> none  [the longest x2 252 us: window_grad(): flat_sum = outer_sum.reshape(chan_width, 2 * tap_count * tap_count)]
    dot_general x7 -> x0, matrix products: 192 us -> none  [the longest x2 94.9 us: window_grad(): jnp.einsum('bic,bjc->cij', blocks, segment, preferred_element_type=jnp.fl...]
    pad x2 -> x0, local copies, waits for them, and re-layouts: 173 us -> none  [window_grad(): flat_sum = jnp.pad(flat_sum, ((0, 0), (0, tap_count)))]
    reduce_sum x2 -> x0, other arithmetic: 44.9 us -> none  [window_grad(): summed = jnp.sum(skewed[:, :, 1:tap_count + 1], axis=1)]
    psum x2 -> x0, blocking collectives: 42.2 us -> none  [window_step(): part_raw, part_norm = lax.psum((part_raw, part_norm), 'chan')]
    gather x1 -> x0, local copies, waits for them, and re-layouts: 35.3 us -> none  [body(): context_rows = query_context[row_index]]
    unnamed x17 -> x0, local copies, waits for them, and re-layouts: 31.9 us -> none
    convert_element_type x1 -> x0, local copies, waits for them, and re-layouts: 23.2 us -> none  [body(): context_rows.astype(jnp.float32)]
  transfers between devices with their start and end apart: 2 -> 3, of which waited for: 1 -> 3; matrix products, arithmetic and copies ran while one was open for 11% -> 0% of each run, Pallas kernels for 0% -> 0%
where the time goes in v1:
time: 35.4 us; the launch traced here: 35.2 us
  Pallas kernels  20.6 us (58%)
  starting transfers between devices  8.15 us (23%)
  waiting for transfers between devices  4.85 us (14%)
  other arithmetic  1.34 us (4%)
    pallas_call x1, Pallas kernels, local_sums(): pl.pallas_call(local_kernel, out_shape=jax.ShapeDtypeStruct((capacity, 12...  20.6 us
    ppermute x3, starting transfers between devices, sum_over(): lax.ppermute(value, axis, [(i, i ^ mask) for i in range(size)])  8.15 us
    ppermute x3, waiting for transfers between devices, sum_over(): lax.ppermute(value, axis, [(i, i ^ mask) for i in range(size)])  4.85 us
  transfers between devices with their start and end apart: 3, of which 3 were waited for; matrix products, arithmetic and copies ran while one was open for 0% of the time, Pallas kernels for 0%

profile of v1, /device:TPU:0, one launch (start us, length us, event | category | flops | bytes accessed | tf_op | source)
XLA Modules:
  0.0 35.2 jit_solution(3068043146439145210)
XLA Ops:
  0.0 20.6 %shard_map.100 = f32[2,128]{1,0:T(2,128)} custom-call(s32[2]{0:T(128)} %counts_hbm.1, s32[64]{0:T(128)} %pos_hbm.1, bf16[2,1024,1024]{2,1,0:T(8,128)(2,1)} %x_hbm.1, bf16[2,1024,1024]{2,1,0:T(8,128)(2,1)} %g_hbm.1, f32[128,128]{1,0:T(8,128)} %basis_hbm.1, f32[1024,128]{1,0:T(8,128)} %eig_hbm.1, bf16[1024,1024]{1,0:T(8,128)(2,1)} %ctx_hbm.1, ...), custom_call_target="tpu_custom_call" | custom-call | flops 4000000000 | bytes 11534336 | tf_op jit(solution)/shard_map/pallas_call | solution.py:221
  20.6 3.0 %collective-permute-start = (f32[2,128]{1,0:T(2,128)}, f32[2,128]{1,0:T(2,128)S(1)}, u32[]{:S(2)}, u32[]{:S(2)}) collective-permute-start(f32[2,128]{1,0:T(2,128)} %shard_map.100), channel_id=1, source_target_pairs={{0,1},{1,0},{2,3},{3,2},{4,5},{5,4},{6,7},{7,6},{8,9},{9,8},{10,11... | collective-permute-start | bytes 3080 | tf_op jit(solution)/shard_map/ppermute | solution.py:261
  23.7 1.8 %collective-permute-done = f32[2,128]{1,0:T(2,128)S(1)} collective-permute-done((f32[2,128]{1,0:T(2,128)}, f32[2,128]{1,0:T(2,128)S(1)}, u32[]{:S(2)}, u32[]{:S(2)}) %collective-permute-start) | collective-permute-done | bytes 1056 | tf_op jit(solution)/shard_map/ppermute | solution.py:261
  25.4 0.7 %add.9 = f32[2,128]{1,0:T(2,128)S(1)} add(f32[2,128]{1,0:T(2,128)} %shard_map.100, f32[2,128]{1,0:T(2,128)S(1)} %collective-permute-done) | non-fusion elementwise | flops 256 | bytes 3072 | tf_op jit(solution)/shard_map/add | solution.py:261
  26.1 2.1 %collective-permute-start.1 = (f32[2,128]{1,0:T(2,128)S(1)}, f32[2,128]{1,0:T(2,128)S(1)}, u32[]{:S(2)}, u32[]{:S(2)}) collective-permute-start(f32[2,128]{1,0:T(2,128)S(1)} %add.9), channel_id=1, source_target_pairs={{0,2},{1,3},{2,0},{3,1},{4,6},{5,7},{6,4},{7,5},{8,10},{9,11},{10,... | collective-permute-start | bytes 3080 | tf_op jit(solution)/shard_map/ppermute | solution.py:261
  28.2 1.5 %collective-permute-done.1 = f32[2,128]{1,0:T(2,128)S(1)} collective-permute-done((f32[2,128]{1,0:T(2,128)S(1)}, f32[2,128]{1,0:T(2,128)S(1)}, u32[]{:S(2)}, u32[]{:S(2)}) %collective-permute-start.1) | collective-permute-done | bytes 1056 | tf_op jit(solution)/shard_map/ppermute | solution.py:261
  29.8 3.0 %collective-permute-start.2 = (f32[2,128]{1,0:T(2,128)S(1)}, f32[2,128]{1,0:T(2,128)S(1)}, u32[]{:S(2)}, u32[]{:S(2)}) collective-permute-start(f32[2,128]{1,0:T(2,128)S(1)} %add.10), channel_id=1, source_target_pairs={{0,4},{1,5},{2,6},{3,7},{4,0},{5,1},{6,2},{7,3},{8,12},{9,13},{10,... | collective-permute-start | bytes 3080 | tf_op jit(solution)/shard_map/ppermute | solution.py:261
  32.8 1.5 %collective-permute-done.2 = f32[2,128]{1,0:T(2,128)S(1)} collective-permute-done((f32[2,128]{1,0:T(2,128)S(1)}, f32[2,128]{1,0:T(2,128)S(1)}, u32[]{:S(2)}, u32[]{:S(2)}) %collective-permute-start.2) | collective-permute-done | bytes 1056 | tf_op jit(solution)/shard_map/ppermute | solution.py:261
  34.3 0.2 sqrt_reduce_fusion
  34.5 0.6 %slice_divide_fusion = f32[2,64]{1,0:T(2,128)} fusion(f32[2,128]{1,0:T(2,128)S(1)} %add.11, f32[2]{0:T(128)S(1)} %sqrt_reduce_fusion), kind=kLoop, calls=%fused_computation.1 | loop fusion | flops 128 | bytes 1032 | tf_op jit(solution)/shard_map/div | solution.py:271
  (2 shorter events, 0.0 us)
Async XLA Ops:
  20.6 4.8 %collective-permute-start = (f32[2,128]{1,0:T(2,128)}, f32[2,128]{1,0:T(2,128)S(1)}, u32[]{:S(2)}, u32[]{:S(2)}) collective-permute-start(f32[2,128]{1,0:T(2,128)} %shard_map.100), channel_id=1, source_target_pairs={{0,1},{1,0},{2,3},{3,2},{4,5},{5,4},{6,7},{7,6},{8,9},{9,8},{10,11... | collective-permute-start | bytes 3080 | tf_op jit(solution)/shard_map/ppermute | solution.py:261
  26.1 3.6 %collective-permute-start.1 = (f32[2,128]{1,0:T(2,128)S(1)}, f32[2,128]{1,0:T(2,128)S(1)}, u32[]{:S(2)}, u32[]{:S(2)}) collective-permute-start(f32[2,128]{1,0:T(2,128)S(1)} %add.9), channel_id=1, source_target_pairs={{0,2},{1,3},{2,0},{3,1},{4,6},{5,7},{6,4},{7,5},{8,10},{9,11},{10,... | collective-permute-start | bytes 3080 | tf_op jit(solution)/shard_map/ppermute | solution.py:261
  29.8 4.6 %collective-permute-start.2 = (f32[2,128]{1,0:T(2,128)S(1)}, f32[2,128]{1,0:T(2,128)S(1)}, u32[]{:S(2)}, u32[]{:S(2)}) collective-permute-start(f32[2,128]{1,0:T(2,128)S(1)} %add.10), channel_id=1, source_target_pairs={{0,4},{1,5},{2,6},{3,7},{4,0},{5,1},{6,2},{7,3},{8,12},{9,13},{10,... | collective-permute-start | bytes 3080 | tf_op jit(solution)/shard_map/ppermute | solution.py:261
